TPU v7x, 128 devices: a whole 4x4x4 slice. The times are simulated.
128 devices in a mesh: node: 4 (over x), surf: 32 (over z, y, core).
Axes of the slice: x: 4, y: 4, z: 4, core: 2. Of those that a mesh axis runs over, the one named last changes fastest.
Arguments:
- sens: bfloat16 [256, 3, 524288], P('node', None, 'surf'), may hold values from -6 to 6
- psi: float32 [35, 256], replicated, may hold values from -4 to 4
- quad_table: float32 [16], replicated, may hold values from 0.004 to 0.04
- quad_index: int32 [256], replicated, may hold values from 0 to 15
- counts: int32 [1024], P('surf'), may hold values from 1 to 512, 327680 in all
- cells: int32 [1024], P('surf'), may hold values from 0 to 383, as said below
- coords: float32 [3, 524288], P(None, 'surf'), may hold values from 0 to 1
Outputs:
- gradient: float32 [105, 24576], P(None, ('node', 'surf'))
Inputs may be any that keep to these rules, and one draw needn't show every extreme that they name: `counts`: some patch is full, with 512 live points, in every draw. `cells`: cell e belongs to owner e // 3. Within each aligned block of 8 patches, no two patches have the same owner.
All inputs are finite; a program needn't handle non-finite values. No bound on the sum of `counts` on one device may be relied on, other than what follows from the above.
Results may differ from a plain program's by a relative error of at most 0.003.
Values may be sent and summed in bfloat16 or wider, within the bound.
No kernel may reach another device: no remote copies, remote signals or barrier semaphores. Data moves between devices by JAX's collectives and lax.ppermute only.
A program may use at most 128 MiB of HBM per device.

v0:
```python
import jax
import jax.numpy as jnp
from jax import lax
from jax.sharding import PartitionSpec as P

K = 35
NQW = 16
CELLS = 384
PATCH_PTS = 512


def bernstein(coords, live):
    one = 1.0 - coords
    basis = jnp.stack(
        [
            one * one * one,
            3.0 * coords * one * one,
            3.0 * coords * coords * one,
            coords * coords * coords,
        ],
        axis=1,
    )
    weights = basis[0][:, None, None, :] * basis[1][None, :, None, :] * basis[2][None, None, :, :]
    return weights.reshape(64, -1) * live[None, :]


def patch_tiles(chaos, counts, coords):
    npatch = counts.shape[0]
    slots = jnp.arange(PATCH_PTS, dtype=jnp.int32)
    live = (slots[None, :] < counts[:, None]).astype(jnp.float32).reshape(-1)
    bern = bernstein(coords, live).reshape(64, npatch, PATCH_PTS)
    flat = chaos.reshape(3 * K, npatch, PATCH_PTS)
    return jnp.einsum("apn,tpn->pat", flat, bern, precision=lax.Precision.HIGHEST)


def dense_lattice(tiles, cells):
    hits = (cells[:, None] == jnp.arange(CELLS, dtype=jnp.int32)[None, :]).astype(jnp.float32)
    spread = jnp.einsum("pe,pat->aet", hits, tiles, precision=lax.Precision.HIGHEST)
    partial_lattice = spread.reshape(3 * K, CELLS * 64)
    return lax.psum_scatter(partial_lattice, ("node", "surf"), scatter_dimension=1, tiled=True)


def local(sens, psi, quad_table, quad_index, counts, cells, coords):
    groups = lax.axis_size("node")
    group_index = lax.axis_index("node")
    hits = (quad_index[:, None] == jnp.arange(NQW, dtype=jnp.int32)[None, :]).astype(jnp.float32)
    qweight = jnp.dot(hits, quad_table, precision=lax.Precision.HIGHEST)
    coef = (psi * qweight[None, :]).astype(jnp.bfloat16)
    quarter_patches = counts.shape[0] // groups
    quarter_points = quarter_patches * PATCH_PTS
    pstart = group_index * quarter_patches
    qstart = group_index * quarter_points
    own_counts = lax.dynamic_slice_in_dim(counts, pstart, quarter_patches, 0)
    own_cells = lax.dynamic_slice_in_dim(cells, pstart, quarter_patches, 0)
    own_coords = lax.dynamic_slice_in_dim(coords, qstart, quarter_points, 1)
    chaos = jnp.einsum(
        "kq,qcn->kcn",
        coef,
        lax.all_to_all(sens, "node", split_axis=2, concat_axis=0, tiled=True),
        preferred_element_type=jnp.float32,
    )
    tiles = patch_tiles(chaos, own_counts, own_coords)
    return dense_lattice(tiles, own_cells)


def solution(mesh):
    in_specs = (P("node", None, "surf"), P(), P(), P(), P("surf"), P("surf"), P(None, "surf"))
    out_specs = P(None, ("node", "surf"))
    return jax.shard_map(local, mesh=mesh, in_specs=in_specs, out_specs=out_specs, check_vma=False)
```

profile of v0, /device:TPU:0, one launch (start us, length us, event | category | flops | bytes accessed | tf_op | source)
XLA Modules:
  0.0 415.6 jit_solution(15547998422458433283)
XLA Ops:
  6.5 0.0 copy-start
  6.5 20.9 %copy.18 = bf16[64,3,16384]{0,1,2:T(4,128)(2,1)} copy(bf16[64,3,16384]{2,0,1:T(8,128)(2,1)} %param.7) | data formatting | bytes 12582912 | tf_op args[0]
  27.5 14.5 %reshape.49 = bf16[4,2,393216]{2,1,0:T(2,128)(2,1)} reshape(bf16[16384,3,64]{2,1,0:T(4,128)(2,1)} %bitcast.37) | data formatting | bytes 12582912
  42.0 0.0 copy-start.4
  42.0 0.0 copy-start.5
  42.0 0.0 copy-start.3
  42.0 5.4 %all-to-all-start = ((bf16[4,2,393216]{2,1,0:T(2,128)(2,1)}), bf16[4,2,393216]{2,1,0:T(2,128)(2,1)}, u32[]{:S(2)}, u32[]{:S(2)}) async-start(bf16[4,2,393216]{2,1,0:T(2,128)(2,1)} %reshape.49), calls=%async_computation | async-start | bytes 12582912 | tf_op jit(solution)/shard_map/all_to_all | solution.py:59
  47.4 0.0 reduce-scatter.2.cloned.1.call-start
  47.4 0.9 fusion.6
  48.3 0.2 pad_maximum_fusion.4
  48.5 0.1 copy_bitcast_fusion
  48.6 0.1 broadcast_multiply_fusion.2
  48.7 0.3 broadcast_multiply_fusion.1
  49.0 0.7 mul.114
  49.7 0.0 copy-done.4
  49.7 0.1 dynamic_slice.10
  49.8 0.0 copy-done.5
  49.8 0.1 dynamic_slice.11
  49.9 0.0 copy-done
  49.9 0.0 copy-done.3
  49.9 0.2 fusion.3
  50.1 0.1 fusion.14
  50.1 0.2 broadcast_multiply_fusion
  50.3 68.5 %all-to-all-done = bf16[4,2,393216]{2,1,0:T(2,128)(2,1)} async-done(((bf16[4,2,393216]{2,1,0:T(2,128)(2,1)}), bf16[4,2,393216]{2,1,0:T(2,128)(2,1)}, u32[]{:S(2)}, u32[]{:S(2)}) %all-to-all-start) | async-done | bytes 6291488 | tf_op jit(solution)/shard_map/all_to_all | solution.py:59
  118.8 13.5 %reshape.50 = bf16[16384,3,64]{2,1,0:T(4,128)(2,1)} reshape(bf16[4,2,393216]{2,1,0:T(2,128)(2,1)} %all-to-all-done) | data formatting | bytes 12582912
  132.3 0.0 copy-start.2
  132.3 21.7 %copy.19 = bf16[64,3,4,4096]{3,0,2,1:T(8,128)(2,1)} copy(bf16[64,3,4,4096]{0,1,3,2:T(4,128)(2,1)} %bitcast.36) | data formatting | bytes 12582912 | tf_op jit(solution)/shard_map/all_to_all | solution.py:59
  154.0 0.0 copy-done.2
  154.0 4.0 fusion.11
  158.0 1.2 copy.20
  159.2 2.5 reshape.43
  161.7 5.1 %fusion = f32[8,105,64]{1,2,0:T(8,128)S(1)} fusion(f32[105,8,512]{2,1,0:T(8,128)} %reshape.43, f32[64,8,512]{2,1,0:T(8,128)S(1)} %broadcast_multiply_fusion), kind=kOutput, calls=%fused_computation.1 | convolution fusion | flops 330301440 | bytes 2983936 | tf_op jit(solution)/shard_map/apn,tpn->pat/dot_general | solution.py:33
  166.8 0.2 copy.23
  167.0 6.9 %convolution_bitcast_fusion = f32[105,384,64]{1,2,0:T(8,128)} fusion(f32[8,105,64]{2,0,1:T(8,128)S(1)} %copy.23, s32[8]{0:T(128)S(1)} %dynamic_slice.11), kind=kOutput, calls=%fused_computation | convolution fusion | flops 247729152 | bytes 10536992 | tf_op jit(solution)/shard_map/pe,pat->aet/dot_general | solution.py:38
  173.9 12.1 %copy.24 = f32[105,384,64]{0,2,1:T(8,128)} copy(f32[105,384,64]{1,2,0:T(8,128)} %convolution_bitcast_fusion) | data formatting | bytes 20643840 | tf_op jit(solution)/shard_map/pe,pat->aet/transpose | solution.py:38
  186.0 0.0 copy-start.1
  186.0 0.0 reduce-scatter.2.cloned.1.call-update
  186.0 222.7 %reduce-scatter.2.cloned.1.call-done = f32[105,192]{0,1:T(8,128)} async-done(((f32[105,24576]{0,1:T(8,128)}), f32[105,192]{0,1:T(8,128)}) %reduce-scatter.2.cloned.1.call-update) | async-done | bytes 80656 | tf_op jit(solution)/shard_map/reduce_scatter | solution.py:40
  408.8 0.0 copy-done.1
  (1 shorter events, 0.0 us)
Async XLA Ops:
  6.5 43.3 %copy-start = (f32[16]{0:T(128)S(1)}, f32[16]{0:T(128)}, u32[]{:S(2)}) copy-start(f32[16]{0:T(128)} %param.9) | copy-start | bytes 196
  42.0 7.7 %copy-start.4 = (s32[32]{0:T(128)S(1)}, s32[32]{0:T(128)}, u32[]{:S(2)}) copy-start(s32[32]{0:T(128)} %param.11) | copy-start | bytes 388
  42.0 7.8 %copy-start.5 = (s32[32]{0:T(128)S(1)}, s32[32]{0:T(128)}, u32[]{:S(2)}) copy-start(s32[32]{0:T(128)} %param.12) | copy-start | bytes 388
  42.0 7.9 %copy-start.3 = (s32[256]{0:T(256)S(1)}, s32[256]{0:T(256)}, u32[]{:S(2)}) copy-start(s32[256]{0:T(256)} %param.10) | copy-start | bytes 3076
  42.0 76.9 %all-to-all-start = ((bf16[4,2,393216]{2,1,0:T(2,128)(2,1)}), bf16[4,2,393216]{2,1,0:T(2,128)(2,1)}, u32[]{:S(2)}, u32[]{:S(2)}) async-start(bf16[4,2,393216]{2,1,0:T(2,128)(2,1)} %reshape.49), calls=%async_computation | async-start | bytes 12582912 | tf_op jit(solution)/shard_map/all_to_all | solution.py:59
  47.4 361.4 %reduce-scatter.2.cloned.1.call-start = ((), (), s32[]{:S(2)}) async-start(), calls=%async_computation.2 | async-start | bytes 12681216 | tf_op jit(solution)/shard_map/reduce_scatter | solution.py:40
  132.3 21.7 %copy-start.2 = (f32[35,256]{1,0:T(8,128)S(1)}, f32[35,256]{1,0:T(8,128)}, u32[]{:S(2)}) copy-start(f32[35,256]{1,0:T(8,128)} %param.8) | copy-start | bytes 107524
  186.0 222.8 %copy-start.1 = (f32[16]{0:T(128)S(1)}, f32[16]{0:T(128)}, u32[]{:S(2)}) copy-start(f32[16]{0:T(128)} %param.9) | copy-start | bytes 196
Sparse Core Ops, SparseCore 0:
  186.1 222.5 reduce-scatter.1
where the time goes:
time: 417 us; the launch traced here: 416 us
  waiting for transfers between devices  291 us (70%)
  local copies, waits for them, and re-layouts  87.6 us (21%)
  matrix products  16.2 us (4%)
  between operations  13.5 us (3%)
  starting transfers between devices  5.43 us (1%)
    reduce_scatter x1, waiting for transfers between devices, dense_lattice(): lax.psum_scatter(partial_lattice, ('node', 'surf'), scatter_dimension=1,...  223 us
    all_to_all x1, waiting for transfers between devices, local(): lax.all_to_all(sens, 'node', split_axis=2, concat_axis=0, tiled=True)  68.5 us
    unnamed x17, local copies, waits for them, and re-layouts  49.1 us
    all_to_all x1, local copies, waits for them, and re-layouts, local(): lax.all_to_all(sens, 'node', split_axis=2, concat_axis=0, tiled=True)  21.7 us
    transpose x1, local copies, waits for them, and re-layouts, dense_lattice(): jnp.einsum('pe,pat->aet', hits, tiles, precision=lax.Precision.HIGHEST)  12.1 us
  transfers between devices with their start and end apart: 2, of which 2 were waited for; matrix products, arithmetic and copies ran while one was open for 1% of the time, Pallas kernels for 0%

commit v1 on v0

--- a/solution.py
+++ b/solution.py
@@ -56,7 +56,10 @@
     chaos = jnp.einsum(
         "kq,qcn->kcn",
         coef,
-        lax.all_to_all(sens, "node", split_axis=2, concat_axis=0, tiled=True),
+        jnp.concatenate(
+            lax.all_to_all(jnp.stack(jnp.split(sens, lax.axis_size("node"), axis=2)), "node", 0, 0),
+            axis=0,
+        ),
         preferred_element_type=jnp.float32,
     )
     tiles = patch_tiles(chaos, own_counts, own_coords)

time: 417 us -> 352 us (0.84)
  local copies, waits for them, and re-layouts: 87.6 us -> 23.5 us
    unnamed x17 -> x12, local copies, waits for them, and re-layouts: 49.1 us -> 0.16 us
    all_to_all x1, local copies, waits for them, and re-layouts: 21.7 us -> 3.21 us  [local(): lax.all_to_all(jnp.stack(jnp.split(sens, lax.axis_size('node'), axis=2)),...]
where the time goes in v1:
time: 352 us
  waiting for transfers between devices  291 us (83%)
  local copies, waits for them, and re-layouts  23.5 us (7%)
  between operations  13.5 us (4%)
  matrix products  13.4 us (4%)
  starting transfers between devices  5.41 us (2%)
  other arithmetic  4.82 us (1%)
    reduce_scatter x1, waiting for transfers between devices, dense_lattice(): lax.psum_scatter(partial_lattice, ('node', 'surf'), scatter_dimension=1,...  223 us
    all_to_all x1, waiting for transfers between devices, local(): lax.all_to_all(jnp.stack(jnp.split(sens, lax.axis_size('node'), axis=2)),...  68.5 us
    transpose x1, local copies, waits for them, and re-layouts, dense_lattice(): jnp.einsum('pe,pat->aet', hits, tiles, precision=lax.Precision.HIGHEST)  12.1 us
  transfers between devices with their start and end apart: 2, of which 2 were waited for; matrix products, arithmetic and copies ran while one was open for 1% of the time, Pallas kernels for 0%

profile of v1, /device:TPU:0, one launch (start us, length us, event | category | flops | bytes accessed | tf_op | source)
XLA Modules:
  0.0 351.9 jit_solution(1548785659387947361)
XLA Ops:
  6.5 0.0 copy-start
  6.5 3.3 slice_bitcast_fusion.3
  9.8 3.2 pad_maximum_fusion
  13.0 0.0 copy-start.3
  13.0 0.0 copy-start.4
  13.0 5.4 %all-to-all-start = ((bf16[4,64,3,4096]{3,1,2,0:T(8,128)(2,1)}), bf16[4,64,3,4096]{3,1,2,0:T(8,128)(2,1)}, u32[]{:S(2)}, u32[]{:S(2)}) async-start(bf16[4,64,3,4096]{3,1,2,0:T(8,128)(2,1)} %pad_maximum_fusion), calls=%async_computation | async-start | bytes 12582912 | tf_op jit(solution)/shard_map/all_to_all | solution.py:60
  18.4 0.0 reduce-scatter.2.cloned.1.call-start
  18.5 0.0 copy-done.3
  18.5 0.1 dynamic_slice.10
  18.6 0.0 copy-done.4
  18.6 0.1 dynamic_slice.11
  18.6 0.9 fusion.6
  19.5 0.0 copy-start.2
  19.5 0.2 pad_maximum_fusion.5
  19.8 0.1 copy_bitcast_fusion
  19.9 0.1 broadcast_multiply_fusion.2
  19.9 0.3 broadcast_multiply_fusion.1
  20.2 0.7 mul.114
  20.9 0.0 copy-done
  20.9 0.0 copy-done.2
  20.9 0.2 fusion.3
  21.1 0.1 fusion.14
  21.2 0.2 broadcast_multiply_fusion
  21.4 0.0 copy-start.1
  21.4 68.5 %all-to-all-done = bf16[4,64,3,4096]{3,1,2,0:T(8,128)(2,1)} async-done(((bf16[4,64,3,4096]{3,1,2,0:T(8,128)(2,1)}), bf16[4,64,3,4096]{3,1,2,0:T(8,128)(2,1)}, u32[]{:S(2)}, u32[]{:S(2)}) %all-to-all-start) | async-done | bytes 6291488 | tf_op jit(solution)/shard_map/all_to_all | solution.py:60
  89.9 3.2 copy.9
  93.1 0.0 copy-done.1
  93.1 1.2 fusion.11
  94.3 1.2 copy.10
  95.5 2.5 reshape.47
  98.0 5.1 %fusion = f32[8,105,64]{1,2,0:T(8,128)S(1)} fusion(f32[105,8,512]{2,1,0:T(8,128)} %reshape.47, f32[64,8,512]{2,1,0:T(8,128)S(1)} %broadcast_multiply_fusion), kind=kOutput, calls=%fused_computation.2 | convolution fusion | flops 330301440 | bytes 2983936 | tf_op jit(solution)/shard_map/apn,tpn->pat/dot_general | solution.py:33
  103.1 0.2 copy.14
  103.3 6.9 %convolution_bitcast_fusion = f32[105,384,64]{1,2,0:T(8,128)} fusion(f32[8,105,64]{2,0,1:T(8,128)S(1)} %copy.14, s32[8]{0:T(128)S(1)} %dynamic_slice.11), kind=kOutput, calls=%fused_computation.1 | convolution fusion | flops 247729152 | bytes 10536992 | tf_op jit(solution)/shard_map/pe,pat->aet/dot_general | solution.py:38
  110.2 12.1 %copy.11 = f32[105,384,64]{0,2,1:T(8,128)} copy(f32[105,384,64]{1,2,0:T(8,128)} %convolution_bitcast_fusion) | data formatting | bytes 20643840 | tf_op jit(solution)/shard_map/pe,pat->aet/transpose | solution.py:38
  122.3 0.0 reduce-scatter.2.cloned.1.call-update
  122.3 222.8 %reduce-scatter.2.cloned.1.call-done = f32[105,192]{0,1:T(8,128)} async-done(((f32[105,24576]{0,1:T(8,128)}), f32[105,192]{0,1:T(8,128)}) %reduce-scatter.2.cloned.1.call-update) | async-done | bytes 80656 | tf_op jit(solution)/shard_map/reduce_scatter | solution.py:40
  (1 shorter events, 0.0 us)
Async XLA Ops:
  6.5 14.4 %copy-start = (f32[16]{0:T(128)S(1)}, f32[16]{0:T(128)}, u32[]{:S(2)}) copy-start(f32[16]{0:T(128)} %param.9) | copy-start | bytes 196
  13.0 5.4 %copy-start.3 = (s32[32]{0:T(128)S(1)}, s32[32]{0:T(128)}, u32[]{:S(2)}) copy-start(s32[32]{0:T(128)} %param.11) | copy-start | bytes 388
  13.0 5.5 %copy-start.4 = (s32[32]{0:T(128)S(1)}, s32[32]{0:T(128)}, u32[]{:S(2)}) copy-start(s32[32]{0:T(128)} %param.12) | copy-start | bytes 388
  13.0 76.8 %all-to-all-start = ((bf16[4,64,3,4096]{3,1,2,0:T(8,128)(2,1)}), bf16[4,64,3,4096]{3,1,2,0:T(8,128)(2,1)}, u32[]{:S(2)}, u32[]{:S(2)}) async-start(bf16[4,64,3,4096]{3,1,2,0:T(8,128)(2,1)} %pad_maximum_fusion), calls=%async_computation | async-start | bytes 12582912 | tf_op jit(solution)/shard_map/all_to_all | solution.py:60
  18.4 326.6 %reduce-scatter.2.cloned.1.call-start = ((), (), s32[]{:S(2)}) async-start(), calls=%async_computation.2 | async-start | bytes 12681216 | tf_op jit(solution)/shard_map/reduce_scatter | solution.py:40
  19.5 1.4 copy-start.2
  21.4 71.7 %copy-start.1 = (f32[35,256]{1,0:T(8,128)S(1)}, f32[35,256]{1,0:T(8,128)}, u32[]{:S(2)}) copy-start(f32[35,256]{1,0:T(8,128)} %param.8) | copy-start | bytes 107524
Sparse Core Ops, SparseCore 0:
  122.4 222.5 reduce-scatter.1
